TPU v7x, 32 devices: a whole 2x2x4 slice. The times are simulated.
32 devices in a mesh: groups: 2 (over y), seq: 4 (over z), head: 2 (over x), sub: 2 (over core).
Axes of the slice: x: 2, y: 2, z: 4, core: 2. Of those that a mesh axis runs over, the one named last changes fastest.
Arguments:
- queries: bfloat16 [2048, 2048], P(('groups', 'seq'), ('head', 'sub')), parts along dimension 0, may hold values from -6 to 6
- keys: bfloat16 [2048, 2048], P(('groups', 'seq'), ('head', 'sub')), parts along dimension 0, may hold values from -0.25 to 0.25
- values: bfloat16 [2048, 2048], P(('groups', 'seq'), ('head', 'sub')), parts along dimension 0, may hold values from -0.75 to 0.75
- out_grad: bfloat16 [2048, 2048], P(('groups', 'seq'), ('head', 'sub')), parts along dimension 0, may hold values from -0.75 to 0.75
- ridge: float32 [16], P(('head', 'sub')), may hold values from 0.8 to 2.4
Outputs:
- mesa_out: float32 [2048, 2048], P(('groups', 'seq'), ('head', 'sub')), parts along dimension 0
- query_grad: float32 [2048, 2048], P(('groups', 'seq'), ('head', 'sub')), parts along dimension 0
- key_grad: float32 [2048, 2048], P(('groups', 'seq'), ('head', 'sub')), parts along dimension 0
- value_grad: float32 [2048, 2048], P(('groups', 'seq'), ('head', 'sub')), parts along dimension 0
There are 2 independent parts, one for each index of `groups`. A program takes and returns all parts, laid end to end along the dimension named above; an argument that names none is the same for every part. Nothing has to cross between parts.
All inputs are finite; a program needn't handle non-finite values.
Results may differ from a plain program's by a relative error of at most 0.0003.
Values sent between devices are 32-bit elements; how exact they have to be, the bound alone decides.
A program may use at most 64 MiB of HBM per device.

v0:
```python
import jax
import jax.numpy as jnp
from jax import lax
from jax.sharding import PartitionSpec as P

HEAD_DIM = 128
BLOCK = 128
CG_STEPS = 4


TINY_VALUE = 1e-30


def carried_in(array, axis, combine, identity, reverse):
    size, position = (lax.axis_size(axis), lax.axis_index(axis))
    everything = jax.tree.map(lambda part: lax.all_gather(part, axis), array)
    start = jax.tree.map(
        lambda part, zero: jnp.broadcast_to(jnp.asarray(zero, part.dtype), part.shape),
        array,
        identity,
    )

    def step(k, before):
        at = size - 1 - k if reverse else k
        reached = at > position if reverse else at < position
        new = combine(before, jax.tree.map(lambda part: part[at], everything))
        return jax.tree.map(lambda a, b: jnp.where(reached, a, b), new, before)

    return lax.fori_loop(0, size, step, start)


def multiply(spec, left, right):
    return jnp.einsum(spec, left, right, precision=lax.Precision.HIGHEST)


def narrow_product(spec, left, right):
    return jnp.einsum(spec, left, right, preferred_element_type=jnp.float32)


def add_pair(earlier, later):
    return (earlier[0] + later[0], earlier[1] + later[1])


def body(queries, keys, values, out_grad, ridge):
    tokens, width = queries.shape
    heads_here = width // HEAD_DIM
    blocks = tokens // BLOCK

    def shape_blocks(array):
        return array.reshape(blocks, BLOCK, heads_here, HEAD_DIM)

    key_b = shape_blocks(keys)
    value_b = shape_blocks(values)
    grad_b = shape_blocks(out_grad)
    query_f = shape_blocks(queries).astype(jnp.float32)
    key_f = key_b.astype(jnp.float32)
    value_f = value_b.astype(jnp.float32)
    grad_f = grad_b.astype(jnp.float32)
    ridge_f = ridge[None, None, :, None]
    positions = jnp.arange(BLOCK)
    lower_mask = (positions[:, None] >= positions[None, :]).astype(jnp.float32)
    upper_mask = lower_mask.T
    key_gram = narrow_product("nchi,nchj->nhij", key_b, key_b)
    value_key = narrow_product("nchi,nchj->nhij", value_b, key_b)
    own_sums = (jnp.sum(key_gram, 0), jnp.sum(value_key, 0))
    zero_state = jnp.zeros_like(own_sums[0])
    gram_in, memory_in = carried_in(
        (own_sums[0], own_sums[1]), "seq", add_pair, (zero_state, zero_state), False
    )
    gram_start = gram_in[None] + jnp.cumsum(key_gram, 0) - key_gram
    memory_start = memory_in[None] + jnp.cumsum(value_key, 0) - value_key

    def apply_op(search):
        scores = multiply("nthd,nshd->nhts", search, key_f) * lower_mask
        return (
            ridge_f * search
            + multiply("nhij,nchj->nchi", gram_start, search)
            + multiply("nhts,nshd->nthd", scores, key_f)
        )

    def conjugate(target):
        solved = jnp.zeros_like(target)
        remain = target
        search = target
        norm_now = jnp.sum(remain * remain, -1, keepdims=True)
        for _ in range(CG_STEPS):
            image = apply_op(search)
            alpha = norm_now / (jnp.sum(search * image, -1, keepdims=True) + TINY_VALUE)
            solved = solved + alpha * search
            remain = remain - alpha * image
            norm_next = jnp.sum(remain * remain, -1, keepdims=True)
            search = remain + norm_next / (norm_now + TINY_VALUE) * search
            norm_now = norm_next
        return solved

    solved = conjugate(query_f)
    attend = multiply("nthd,nshd->nhts", solved, key_f) * lower_mask
    output = multiply("nhij,nchj->nchi", memory_start, solved) + multiply(
        "nhts,nshd->nthd", attend, value_f
    )
    grad_scores = narrow_product("nthd,nshd->nhts", grad_b, value_b) * lower_mask
    pulled = multiply("nhij,nchi->nchj", memory_start, grad_f) + multiply(
        "nhts,nshd->nthd", grad_scores, key_f
    )
    adjoint = conjugate(pulled)
    cross = multiply("nchi,nchj->nhij", adjoint, solved)
    pair_block = cross + jnp.transpose(cross, (0, 1, 3, 2))
    grad_block = multiply("nchi,nchj->nhij", grad_f, solved)
    own_back = (jnp.sum(pair_block, 0), jnp.sum(grad_block, 0))
    pair_in, grad_in = carried_in(
        (own_back[0], own_back[1]), "seq", add_pair, (zero_state, zero_state), True
    )
    pair_end = pair_in[None] + jnp.cumsum(pair_block[::-1], 0)[::-1] - pair_block
    grad_end = grad_in[None] + jnp.cumsum(grad_block[::-1], 0)[::-1] - grad_block
    key_solved = multiply("nihd,nthd->nhit", key_f, solved) * upper_mask
    key_adjoint = multiply("nihd,nthd->nhit", key_f, adjoint) * upper_mask
    value_scores = narrow_product("nihd,nthd->nhit", value_b, grad_b) * upper_mask
    key_out = (
        -(
            multiply("nhij,nchj->nchi", pair_end, key_f)
            + multiply("nhit,nthd->nihd", key_solved, adjoint)
            + multiply("nhit,nthd->nihd", key_adjoint, solved)
        )
        + multiply("nhij,nchi->nchj", grad_end, value_f)
        + multiply("nhit,nthd->nihd", value_scores, solved)
    )
    value_out = multiply("nhij,nchj->nchi", grad_end, key_f) + multiply(
        "nhit,nthd->nihd", key_solved, grad_f
    )

    def merge_back(array):
        return array.reshape(tokens, width)

    return (merge_back(output), merge_back(adjoint), merge_back(key_out), merge_back(value_out))


def solution(mesh):
    in_specs = (
        P(("groups", "seq"), ("head", "sub")),
        P(("groups", "seq"), ("head", "sub")),
        P(("groups", "seq"), ("head", "sub")),
        P(("groups", "seq"), ("head", "sub")),
        P(("head", "sub")),
    )
    out_specs = (
        P(("groups", "seq"), ("head", "sub")),
        P(("groups", "seq"), ("head", "sub")),
        P(("groups", "seq"), ("head", "sub")),
        P(("groups", "seq"), ("head", "sub")),
    )
    return jax.shard_map(body, mesh=mesh, in_specs=in_specs, out_specs=out_specs, check_vma=False)
```

profile of v0, /device:TPU:0, one launch (start us, length us, event | category | flops | bytes accessed | tf_op | source)
XLA Modules:
  0.0 176.1 jit_solution(13642010963612374477)
XLA Ops:
  7.2 1.0 reshape.176
  8.4 0.9 fusion.77
  9.4 0.9 copy-done.11
  10.4 1.0 fusion.78
  11.5 0.8 copy-done.12
  12.6 0.7 copy-done.13
  14.1 1.5 convolution_bitcast_fusion.13
  15.5 0.7 convolution_bitcast_fusion.8
  16.2 24.6 %all-gather.9.cloned.1.call-done = f32[16,128,128]{2,1,0:T(8,128)} async-done(((f32[4,128,128]{2,1,0:T(8,128)}), f32[16,128,128]{2,1,0:T(8,128)}) %all-gather.9.cloned.1.call-update) | async-done | bytes 1048592 | tf_op jit(solution)/shard_map/all_gather | solution.py:16
  40.8 29.6 %all-gather.11.cloned.1.call-done = f32[16,128,128]{2,1,0:T(8,128)} async-done(((f32[4,128,128]{2,1,0:T(8,128)}), f32[16,128,128]{2,1,0:T(8,128)}) %all-gather.11.cloned.1.call-update) | async-done | bytes 1048592 | tf_op jit(solution)/shard_map/all_gather | solution.py:16
  70.4 5.0 %while.34 = (s32[]{:T(128)}, f32[4,128,128]{2,1,0:T(8,128)S(1)}, f32[4,128,128]{2,1,0:T(8,128)S(1)}, s32[]{:T(128)}, f32[4,4,128,128]{3,2,1,0:T(8,128)}, /*index=5*/f32[4,4,128,128]{3,2,1,0:T(8,128)}, s32[]{:T(128)}, s32[]{:T(128)}) while((s32[]{:T(128)}, f32[4,128,128]{2,1,0:T(8,128)S(1)}, f32[4,128,128]{2,1,0:T(8,128)S(1)}, ...), condition=%wide.region_4.5_spmd.clone, body=%wide.region_3.4_spmd.clone.sunk | while | flops 393220 | bytes 1572973 | solution.py:29
  70.4 1.2 add_select_fusion.6
  71.7 1.2 add_select_fusion.6
  72.9 1.2 add_select_fusion.6
  74.2 1.2 add_select_fusion.6
  75.6 0.9 copy-done.9
  78.4 0.8 multiply_reduce_fusion.10
  80.8 0.7 multiply_reduce_fusion.8
  83.0 0.7 fusion.27
  86.3 0.7 multiply_reduce_fusion.5
  88.5 0.7 multiply_reduce_fusion.3
  90.7 0.7 multiply_reduce_fusion.1
  93.8 1.2 fusion.82
  95.0 1.0 copy.145
  96.0 1.8 %fusion.76 = (f32[4,128,128]{2,1,0:T(8,128)}, f32[2,4,128,128]{3,2,1,0:T(8,128)S(1)}) fusion(f32[2,4,128,128]{3,2,1,0:T(8,128)S(1)} %fusion.82, f32[2,4,128,128]{2,3,1,0:T(8,128)} %copy.145), kind=kLoop, calls=%fused_computation.168 | loop fusion | flops 196608 | bytes 1835008 | tf_op jit(solution)/shard_map/reduce_sum | solution.py:109
  97.9 1.1 convolution_multiply_fusion
  99.0 1.0 copy.143
  100.5 0.8 rev.13
  101.7 0.9 copy.147
  102.6 0.8 rev.14
  105.1 1.0 fusion.5
  106.5 0.7 copy-done.6
  107.2 0.8 fusion.81
  108.0 1.4 fusion.25
  109.4 1.2 convolution_bitcast_fusion
  110.7 1.0 copy_bitcast_fusion.2
  111.7 13.7 %all-gather.13.cloned.1.call-done = f32[16,128,128]{2,1,0:T(8,128)} async-done(((f32[4,128,128]{2,1,0:T(8,128)}), f32[16,128,128]{2,1,0:T(8,128)}) %all-gather.13.cloned.1.call-update) | async-done | bytes 1048592 | tf_op jit(solution)/shard_map/all_gather | solution.py:16
  125.4 28.9 %all-gather.15.cloned.1.call-done = f32[16,128,128]{2,1,0:T(8,128)} async-done(((f32[4,128,128]{2,1,0:T(8,128)}), f32[16,128,128]{2,1,0:T(8,128)}) %all-gather.15.cloned.1.call-update) | async-done | bytes 1048592 | tf_op jit(solution)/shard_map/all_gather | solution.py:16
  154.3 5.0 %while.35 = (s32[]{:T(128)}, f32[4,128,128]{2,1,0:T(8,128)S(1)}, f32[4,128,128]{2,1,0:T(8,128)S(1)}, s32[]{:T(128)}, f32[4,4,128,128]{3,2,1,0:T(8,128)}, /*index...) while((s32[]{:T(128)}, f32[4,128,128]{2,1,0:T(8,128)S(1)}, ...), condition=%wide.region_25.26_spmd.clone, body=%wide.region_24.25_spmd.clone.sunk | while | flops 393224 | bytes 1573035 | solution.py:29
  154.3 1.2 add_select_fusion.7
  155.5 1.2 add_select_fusion.7
  156.8 1.2 add_select_fusion.7
  158.1 1.2 add_select_fusion.7
  159.3 1.9 %fusion.35 = f32[2,4,128,128]{3,2,1,0:T(8,128)S(1)} fusion(f32[2,4,128,128]{3,2,1,0:T(8,128)} %copy-done.2, f32[2,4,128,128]{3,2,1,0:T(8,128)} %rev.13, f32[4,128,128]{2,1,0:T(8,128)S(1)} %get-tuple-element.271, bf16[2,128,4,128]{3,2,1,0:T(4,128)(2,1)S(1)} %reshape.176), kind=kOutput, calls=%fused_computation.90 | convolution fusion | flops 201588736 | bytes 2097152 | tf_op jit(solution)/shard_map/nhij,nchj->nchi/dot_general | solution.py:33
  161.2 1.4 convolution_add_fusion.2
  162.7 0.9 copy-done.5
  166.9 0.8 copy-done.3
  168.5 1.0 copy_bitcast_fusion
  (104 shorter events, 21.4 us)
Async XLA Ops:
  7.2 33.6 %all-gather.9.cloned.1.call-start = ((), (), s32[]{:S(2)}) async-start(), calls=%async_computation | async-start | bytes 1310720 | tf_op jit(solution)/shard_map/all_gather | solution.py:16
  9.4 0.9 copy-start.11
  9.4 61.0 %all-gather.11.cloned.1.call-start = ((), (), s32[]{:S(2)}) async-start(), calls=%async_computation.1 | async-start | bytes 1310720 | tf_op jit(solution)/shard_map/all_gather | solution.py:16
  11.4 0.9 copy-start.12
  11.4 114.0 %all-gather.13.cloned.1.call-start = ((), (), s32[]{:S(2)}) async-start(), calls=%async_computation.2 | async-start | bytes 1310720 | tf_op jit(solution)/shard_map/all_gather | solution.py:16
  12.4 1.0 copy-start.13
  75.4 1.0 copy-start.9
  75.4 1.0 copy-start.14
  84.2 0.8 copy-start
  97.8 2.2 %copy-start.2 = (f32[2,4,128,128]{3,2,1,0:T(8,128)}, f32[2,4,128,128]{3,2,1,0:T(8,128)S(1)}, u32[]{:S(2)}) copy-start(f32[2,4,128,128]{3,2,1,0:T(8,128)S(1)} %get-tuple-element.344) | copy-start | bytes 1572868
  97.8 56.5 %all-gather.15.cloned.1.call-start = ((), (), s32[]{:S(2)}) async-start(), calls=%async_computation.3 | async-start | bytes 1310720 | tf_op jit(solution)/shard_map/all_gather | solution.py:16
  104.0 1.1 copy-start.1
  106.1 1.0 copy-start.6
  109.4 1.3 copy-start.10
  162.6 1.0 copy-start.5
  163.7 1.0 copy-start.4
  163.7 1.2 copy-start.7
  164.9 1.0 copy-start.8
  166.6 1.0 copy-start.3
Sparse Core Ops, SparseCore 0:
  10.1 30.6 all-gather.8
  42.9 27.4 all-gather.10
  98.0 27.4 all-gather.12
  126.8 27.4 all-gather.14
where the time goes:
time: 177 us; the launch traced here: 176 us
  waiting for transfers between devices  96.9 us (55%)
  matrix products  32.7 us (18%)
  local copies, waits for them, and re-layouts  16.6 us (9%)
  other arithmetic  15.2 us (9%)
  between operations  14.4 us (8%)
    all_gather x4, waiting for transfers between devices, carried_in(): everything = jax.tree.map(lambda part: lax.all_gather(part, axis), array)  96.8 us
    dot_general x39, matrix products, multiply(): return jnp.einsum(spec, left, right, precision=lax.Precision.HIGHEST)  29.4 us
    select_n x8, other arithmetic, step(): return jax.tree.map(lambda a, b: jnp.where(reached, a, b), new, before)  9.8 us
    unnamed x30, local copies, waits for them, and re-layouts  7.48 us
  transfers between devices with their start and end apart: 4, of which 4 were waited for; matrix products, arithmetic and copies ran while one was open for 9% of the time, Pallas kernels for 0%

commit v1 on v0

v1 whole, which is shorter than its diff:
```python
import functools

import jax
import jax.numpy as jnp
from jax import lax
from jax.experimental import pallas as pl
from jax.experimental.pallas import tpu as pltpu
from jax.sharding import PartitionSpec as P

D = 128
CG_STEPS = 4
TINY = 1e-30
F32 = jnp.float32
BF16 = jnp.bfloat16
MESH = pl.DeviceIdType.MESH


def split(a):
    hi = a.astype(BF16)
    lo = (a - hi.astype(F32)).astype(BF16)
    return hi, lo


def dot(a, b):
    return jnp.dot(a, b, preferred_element_type=F32)


def dot_t(a, b):
    return lax.dot_general(a, b, (((1,), (1,)), ((), ())), preferred_element_type=F32)


def colsum(a):
    return jnp.sum(a, axis=0, keepdims=True)


def kernel(n, heads, ridge_ref, q_ref, k_ref, v_ref, g_ref,
           out_ref, qg_ref, kg_ref, vg_ref,
           kt_ref, vt_ref, gt_ref, fown, fin, rown, rin,
           fsend, frecv, rsend, rrecv):
    z = lax.axis_index("seq")
    tokens = q_ref.shape[0]
    barrier = pltpu.get_barrier_semaphore()

    @pl.when(z > 0)
    def _():
        pl.semaphore_signal(barrier, inc=1, device_id={"seq": z - 1}, device_id_type=MESH)

    @pl.when(z < n - 1)
    def _():
        pl.semaphore_signal(barrier, inc=1, device_id={"seq": z + 1}, device_id_type=MESH)

    def cols(h):
        return pl.ds(pl.multiple_of(h * D, D), D)

    def fcopy(h, c):
        return pltpu.make_async_remote_copy(
            src_ref=fown.at[h, c], dst_ref=fin.at[h, c],
            send_sem=fsend.at[h, c], recv_sem=frecv.at[h, c],
            device_id={"seq": z + 1}, device_id_type=MESH)

    def rcopy(h, c):
        return pltpu.make_async_remote_copy(
            src_ref=rown.at[h, c], dst_ref=rin.at[h, c],
            send_sem=rsend.at[h, c], recv_sem=rrecv.at[h, c],
            device_id={"seq": z - 1}, device_id_type=MESH)

    @pl.when(z == 0)
    def _():
        fin[...] = jnp.zeros_like(fin)

    @pl.when(z == n - 1)
    def _():
        rin[...] = jnp.zeros_like(rin)

    def own(h, _):
        c = cols(h)
        k = k_ref[:, c]
        kt = k.astype(F32).T.astype(BF16)
        vt = v_ref[:, c].astype(F32).T.astype(BF16)
        kt_ref[h] = kt
        vt_ref[h] = vt
        gt_ref[h] = g_ref[:, c].astype(F32).T.astype(BF16)
        fown[h, 0] = dot(kt, k)
        fown[h, 1] = dot(vt, k)
        return 0

    lax.fori_loop(0, heads, own, 0)

    @pl.when((z > 0) & (z < n - 1))
    def _():
        pl.semaphore_wait(barrier, 2)

    @pl.when((z == 0) | (z == n - 1))
    def _():
        pl.semaphore_wait(barrier, 1)

    @pl.when(z == 0)
    def _():
        for h in range(heads):
            for c in range(2):
                fcopy(h, c).start()

    srow = lax.broadcasted_iota(jnp.int32, (tokens, tokens), 0)
    tcol = lax.broadcasted_iota(jnp.int32, (tokens, tokens), 1)
    mask = srow <= tcol

    def forward(h, _):
        for c in range(2):
            @pl.when(z > 0)
            def _():
                fcopy(h, c).wait_recv()

            @pl.when((z > 0) & (z < n - 1))
            def _():
                fown[h, c] = fown[h, c] + fin[h, c]
                fcopy(h, c).start()

        c = cols(h)
        k = k_ref[:, c]
        v = v_ref[:, c]
        kt = kt_ref[h]
        vt = vt_ref[h]
        gt = gt_ref[h]
        ridge = ridge_ref[h]
        kk = jnp.concatenate([k, k], axis=1)
        ghi, glo = split(fin[h, 0])
        gg = jnp.concatenate([ghi, ghi], axis=1)
        m = fin[h, 1]
        mhi, mlo = split(m)
        mm = jnp.concatenate([mhi, mhi], axis=1)
        mt = m.T
        mthi, mtlo = split(mt)

        vs = jnp.where(mask, dot(v, gt), 0.0)
        vh, vl = split(vs)
        pulled = dot(kt, vh) + dot(kt, vl) + dot(mthi, gt) + dot(mtlo, gt)
        query = q_ref[:, c].astype(F32).T

        def scores(ph, pp):
            return jnp.where(mask, dot(kk, pp), 0.0)

        state = []
        for b in (query, pulled):
            state.append([None, b, b, colsum(b * b)])
        for step in range(CG_STEPS):
            for one in state:
                s, r, p, rho = one
                ph, pl_ = split(p)
                pp = jnp.concatenate([ph, pl_], axis=0)
                sc = scores(ph, pp)
                gp = dot(gg, pp) + dot(glo, ph)
                if step < CG_STEPS - 1:
                    sh, sl = split(sc)
                    w = ridge * p + gp + dot(kt, sh) + dot(kt, sl)
                    alpha = rho / (colsum(p * w) + TINY)
                    s = alpha * p if s is None else s + alpha * p
                    r = r - alpha * w
                    rho2 = colsum(r * r)
                    p = r + (rho2 / (rho + TINY)) * p
                    one[:] = [s, r, p, rho2]
                else:
                    pw = colsum(p * (ridge * p + gp)) + colsum(sc * sc)
                    one[0] = s + (rho / (pw + TINY)) * p

        x, y = state[0][0], state[1][0]
        qg_ref[:, c] = y.T
        xh, xl = split(x)
        yh, yl = split(y)
        xx = jnp.concatenate([xh, xl], axis=0)
        yy = jnp.concatenate([yh, yl], axis=0)

        cross = dot_t(yh, xh) + dot_t(yl, xh) + dot_t(yh, xl)
        rown[h, 0] = cross + cross.T
        rown[h, 1] = dot_t(gt, xh) + dot_t(gt, xl)

        @pl.when(z == n - 1)
        def _():
            for c2 in range(2):
                rcopy(h, c2).start()

        ks = scores(xh, xx)
        ah, al = split(ks)
        out = dot(mm, xx) + dot(mlo, xh) + dot(vt, ah) + dot(vt, al)
        out_ref[:, c] = out.T
        ka = scores(yh, yy) - vs
        bh, bl = split(ka)
        kg_ref[:, c] = -(dot_t(ah, yh) + dot_t(al, yh) + dot_t(ah, yl)
                         + dot_t(bh, xh) + dot_t(bl, xh) + dot_t(bh, xl))
        vg_ref[:, c] = dot_t(ah, gt) + dot_t(al, gt)
        return 0

    lax.fori_loop(0, heads, forward, 0)

    def backward(h, _):
        for c in range(2):
            @pl.when(z < n - 1)
            def _():
                rcopy(h, c).wait_recv()

            @pl.when((z > 0) & (z < n - 1))
            def _():
                rown[h, c] = rown[h, c] + rin[h, c]
                rcopy(h, c).start()

        c = cols(h)
        k = k_ref[:, c]
        v = v_ref[:, c]
        ph, pl_ = split(rin[h, 0])
        qh, ql = split(rin[h, 1])
        kg_ref[:, c] = kg_ref[:, c] + (dot(v, qh) + dot(v, ql)) - (dot(k, ph) + dot(k, pl_))
        vg_ref[:, c] = vg_ref[:, c] + (dot_t(k, qh) + dot_t(k, ql))
        return 0

    lax.fori_loop(0, heads, backward, 0)

    for h in range(heads):
        for c in range(2):
            @pl.when(z < n - 1)
            def _():
                fcopy(h, c).wait_send()

            @pl.when(z > 0)
            def _():
                rcopy(h, c).wait_send()


def body(n, queries, keys, values, out_grad, ridge):
    tokens, width = queries.shape
    heads = width // D
    vm = pl.BlockSpec(memory_space=pltpu.VMEM)
    out = jax.ShapeDtypeStruct((tokens, width), F32)
    return pl.pallas_call(
        functools.partial(kernel, n, heads),
        out_shape=[out] * 4,
        in_specs=[pl.BlockSpec(memory_space=pltpu.SMEM)] + [vm] * 4,
        out_specs=[vm] * 4,
        scratch_shapes=[
            pltpu.VMEM((heads, D, tokens), BF16),
            pltpu.VMEM((heads, D, tokens), BF16),
            pltpu.VMEM((heads, D, tokens), BF16),
            pltpu.VMEM((heads, 2, D, D), F32),
            pltpu.VMEM((heads, 2, D, D), F32),
            pltpu.VMEM((heads, 2, D, D), F32),
            pltpu.VMEM((heads, 2, D, D), F32),
            pltpu.SemaphoreType.DMA((heads, 2)),
            pltpu.SemaphoreType.DMA((heads, 2)),
            pltpu.SemaphoreType.DMA((heads, 2)),
            pltpu.SemaphoreType.DMA((heads, 2)),
        ],
        compiler_params=pltpu.CompilerParams(
            collective_id=0, has_side_effects=True, vmem_limit_bytes=40 * 2**20),
        name="mesa",
    )(ridge, queries, keys, values, out_grad)


def solution(mesh):
    spec = P(("groups", "seq"), ("head", "sub"))
    return jax.shard_map(
        functools.partial(body, mesh.shape["seq"]), mesh=mesh,
        in_specs=(spec, spec, spec, spec, P(("head", "sub"))),
        out_specs=(spec, spec, spec, spec), check_vma=False)
```

time: 177 us -> 49.7 us (0.28)
  waiting for transfers between devices: 96.9 us -> 0 us
  Pallas kernels: 0 us -> 41.2 us
  matrix products: 32.7 us -> 0 us
  other arithmetic: 15.2 us -> 0 us
  between operations: 14.4 us -> 0.65 us
  local copies, waits for them, and re-layouts: 16.6 us -> 7.62 us
    all_gather x4 -> x0, waiting for transfers between devices: 96.8 us -> none  [carried_in(): everything = jax.tree.map(lambda part: lax.all_gather(part, axis), array)]
    pallas_call x0 -> x1, Pallas kernels: none -> 41.2 us  [body(): pl.pallas_call(functools.partial(kernel, n, heads), out_shape=[out] * 4,...]
    dot_general x43 -> x0, matrix products: 32.7 us -> none  [the longest x39 29.4 us: multiply(): return jnp.einsum(spec, left, right, precision=lax.Precision.HIGHEST)]
    select_n x8 -> x0, other arithmetic: 9.8 us -> none  [step(): return jax.tree.map(lambda a, b: jnp.where(reached, a, b), new, before)]
    reshape x8 -> x0, local copies, waits for them, and re-layouts: 3.66 us -> none  [the longest x2 2.07 us: merge_back(): return array.reshape(tokens, width)]
    reduce_sum x7 -> x0, other arithmetic: 2.51 us -> none  [the longest x1 1.85 us: body(): own_back = (jnp.sum(pair_block, 0), jnp.sum(grad_block, 0))]
    add x4 -> x0, local copies, waits for them, and re-layouts: 1.8 us -> none  [the longest x1 0.99 us: conjugate(): solved = solved + alpha * search]
    another operation x4 -> x0, other arithmetic: 1.78 us -> none  [the longest x1 0.85 us: body(): jnp.cumsum(grad_block[::-1], 0)[::-1]]
  transfers between devices with their start and end apart: 4 -> 0, of which waited for: 4 -> 0; matrix products, arithmetic and copies ran while one was open for 9% -> 0% of each run, Pallas kernels for 0% -> 0%
where the time goes in v1:
time: 49.7 us; the launch traced here: 49.5 us
  Pallas kernels  41.2 us (83%)
  local copies, waits for them, and re-layouts  7.62 us (15%)
  between operations  0.65 us (1%)
    pallas_call x1, Pallas kernels, body(): pl.pallas_call(functools.partial(kernel, n, heads), out_shape=[out] * 4,...  41.2 us
    unnamed x14, local copies, waits for them, and re-layouts  7.62 us

profile of v1, /device:TPU:0, one launch (start us, length us, event | category | flops | bytes accessed | tf_op | source)
XLA Modules:
  0.0 49.5 jit_solution(17075360146527014669)
XLA Ops:
  0.6 0.0 copy-start
  0.6 0.9 %copy-done = bf16[256,512]{1,0:T(8,128)(2,1)S(1)} copy-done((bf16[256,512]{1,0:T(8,128)(2,1)S(1)}, bf16[256,512]{1,0:T(8,128)(2,1)}, u32[]{:S(2)}) %copy-start) | copy-done | bytes 262168
  1.6 0.0 copy-start.1
  1.6 0.9 %copy-done.1 = bf16[256,512]{1,0:T(8,128)(2,1)S(1)} copy-done((bf16[256,512]{1,0:T(8,128)(2,1)S(1)}, bf16[256,512]{1,0:T(8,128)(2,1)}, u32[]{:S(2)}) %copy-start.1) | copy-done | bytes 262168
  2.5 0.0 copy-start.2
  2.5 0.9 %copy-done.2 = bf16[256,512]{1,0:T(8,128)(2,1)S(1)} copy-done((bf16[256,512]{1,0:T(8,128)(2,1)S(1)}, bf16[256,512]{1,0:T(8,128)(2,1)}, u32[]{:S(2)}) %copy-start.2) | copy-done | bytes 262168
  3.5 0.0 copy-start.3
  3.5 0.9 %copy-done.3 = bf16[256,512]{1,0:T(8,128)(2,1)S(1)} copy-done((bf16[256,512]{1,0:T(8,128)(2,1)S(1)}, bf16[256,512]{1,0:T(8,128)(2,1)}, u32[]{:S(2)}) %copy-start.3) | copy-done | bytes 262168
  4.4 0.0 copy-start.4
  4.4 0.7 %copy-done.4 = f32[4]{0:T(128)S(1)} copy-done((f32[4]{0:T(128)S(1)}, f32[4]{0:T(128)}, u32[]{:S(2)}) %copy-start.4) | copy-done | bytes 40
  5.1 41.2 %mesa.1 = (f32[256,512]{1,0:T(8,128)S(1)}, f32[256,512]{1,0:T(8,128)S(1)}, f32[256,512]{1,0:T(8,128)S(1)}, f32[256,512]{1,0:T(8,128)S(1)}) custom-call(f32[4]{0:T(128)S(1)} %copy-done.4, bf16[256,512]{1,0:T(8,128)(2,1)S(1)} %copy-done, bf16[256,512]{1,0:T(8,128)(2,1)S(1)} %copy-done.1, bf16[256,512]{1,0:T(8,128)(2,1)S(1)} %copy-done.2, ...), custom_call_target="tpu_custom_call" | custom-call | tf_op jit(solution)/shard_map/mesa/pallas_call | solution.py:232
  46.3 0.8 %copy.13 = f32[256,512]{1,0:T(8,128)} copy(f32[256,512]{1,0:T(8,128)S(1)} %get-tuple-element.8) | data formatting | bytes 1048576
  47.1 0.8 %copy.14 = f32[256,512]{1,0:T(8,128)} copy(f32[256,512]{1,0:T(8,128)S(1)} %get-tuple-element.9) | data formatting | bytes 1048576
  47.9 0.8 %copy.15 = f32[256,512]{1,0:T(8,128)} copy(f32[256,512]{1,0:T(8,128)S(1)} %get-tuple-element.10) | data formatting | bytes 1048576
  48.7 0.8 %copy.16 = f32[256,512]{1,0:T(8,128)} copy(f32[256,512]{1,0:T(8,128)S(1)} %get-tuple-element.11) | data formatting | bytes 1048576
Async XLA Ops:
  0.6 1.0 %copy-start = (bf16[256,512]{1,0:T(8,128)(2,1)S(1)}, bf16[256,512]{1,0:T(8,128)(2,1)}, u32[]{:S(2)}) copy-start(bf16[256,512]{1,0:T(8,128)(2,1)} %q_ref.1) | copy-start | bytes 786436
  1.6 0.9 %copy-start.1 = (bf16[256,512]{1,0:T(8,128)(2,1)S(1)}, bf16[256,512]{1,0:T(8,128)(2,1)}, u32[]{:S(2)}) copy-start(bf16[256,512]{1,0:T(8,128)(2,1)} %k_ref.1) | copy-start | bytes 786436
  2.5 0.9 %copy-start.2 = (bf16[256,512]{1,0:T(8,128)(2,1)S(1)}, bf16[256,512]{1,0:T(8,128)(2,1)}, u32[]{:S(2)}) copy-start(bf16[256,512]{1,0:T(8,128)(2,1)} %v_ref.1) | copy-start | bytes 786436
  3.5 0.9 %copy-start.3 = (bf16[256,512]{1,0:T(8,128)(2,1)S(1)}, bf16[256,512]{1,0:T(8,128)(2,1)}, u32[]{:S(2)}) copy-start(bf16[256,512]{1,0:T(8,128)(2,1)} %g_ref.1) | copy-start | bytes 786436
  4.4 0.7 %copy-start.4 = (f32[4]{0:T(128)S(1)}, f32[4]{0:T(128)}, u32[]{:S(2)}) copy-start(f32[4]{0:T(128)} %ridge_ref.1) | copy-start | bytes 52

commit v2 on v1

--- a/solution.py
+++ b/solution.py
@@ -9,6 +9,7 @@
 
 D = 128
 CG_STEPS = 4
+LAG = 2
 TINY = 1e-30
 F32 = jnp.float32
 BF16 = jnp.bfloat16
@@ -33,12 +34,45 @@
     return jnp.sum(a, axis=0, keepdims=True)
 
 
-def kernel(n, heads, ridge_ref, q_ref, k_ref, v_ref, g_ref,
+H = D // 2
+ROWS = H + 8 + D
+CHUNKS = ((0, H + 8), (H + 8, H), (D + 8, H))
+
+
+def iotas(shape):
+    return lax.broadcasted_iota(jnp.int32, shape, 0), lax.broadcasted_iota(jnp.int32, shape, 1)
+
+
+def pack(ref, a):
+    r, c = iotas((H, D))
+    top = a[:H]
+    bot = pltpu.roll(a[H:], H, axis=1)
+    ref[:H] = jnp.where((c < H) & (c > r), bot, top)
+    ref[H:H + 8] = jnp.broadcast_to(colsum(jnp.where(c == r, bot, 0.0)), (8, D))
+
+
+def unpack(ref):
+    r, c = iotas((H, D))
+    b = ref[:H]
+    diag = ref[H:H + 8][:1]
+    t = jnp.concatenate([b, jnp.zeros_like(b)], axis=0).T
+    tl = t[:H]
+    top = jnp.where((c < H) & (c > r), tl, b)
+    low = jnp.where(c > r, b, jnp.where(c < r, tl, diag))
+    bot = jnp.where(c < H, t[H:], pltpu.roll(low, H, axis=1))
+    return jnp.concatenate([top, bot], axis=0)
+
+
+def kernel(n, heads, ridge_ref, q_hbm, k_hbm, v_hbm, g_hbm,
            out_ref, qg_ref, kg_ref, vg_ref,
-           kt_ref, vt_ref, gt_ref, fown, fin, rown, rin,
+           q_ref, k_ref, v_ref, g_ref, load, kt_ref, vt_ref, fown, fin, rown, rin,
            fsend, frecv, rsend, rrecv):
     z = lax.axis_index("seq")
     tokens = q_ref.shape[0]
+    loads = [pltpu.make_async_copy(a, b, load.at[i]) for i, (a, b) in enumerate(
+        ((k_hbm, k_ref), (v_hbm, v_ref), (g_hbm, g_ref), (q_hbm, q_ref)))]
+    for one in loads:
+        one.start()
     barrier = pltpu.get_barrier_semaphore()
 
     @pl.when(z > 0)
@@ -52,15 +86,18 @@
     def cols(h):
         return pl.ds(pl.multiple_of(h * D, D), D)
 
+    def part(c):
+        return pl.ds(*CHUNKS[c])
+
     def fcopy(h, c):
         return pltpu.make_async_remote_copy(
-            src_ref=fown.at[h, c], dst_ref=fin.at[h, c],
+            src_ref=fown.at[h, part(c)], dst_ref=fin.at[h, part(c)],
             send_sem=fsend.at[h, c], recv_sem=frecv.at[h, c],
             device_id={"seq": z + 1}, device_id_type=MESH)
 
     def rcopy(h, c):
         return pltpu.make_async_remote_copy(
-            src_ref=rown.at[h, c], dst_ref=rin.at[h, c],
+            src_ref=rown.at[h, part(c)], dst_ref=rin.at[h, part(c)],
             send_sem=rsend.at[h, c], recv_sem=rrecv.at[h, c],
             device_id={"seq": z - 1}, device_id_type=MESH)
 
@@ -79,11 +116,12 @@
         vt = v_ref[:, c].astype(F32).T.astype(BF16)
         kt_ref[h] = kt
         vt_ref[h] = vt
-        gt_ref[h] = g_ref[:, c].astype(F32).T.astype(BF16)
-        fown[h, 0] = dot(kt, k)
-        fown[h, 1] = dot(vt, k)
+        pack(fown.at[h], dot(kt, k))
+        fown[h, H + 8:] = dot(vt, k)
         return 0
 
+    loads[0].wait()
+    loads[1].wait()
     lax.fori_loop(0, heads, own, 0)
 
     @pl.when((z > 0) & (z < n - 1))
@@ -97,22 +135,45 @@
     @pl.when(z == 0)
     def _():
         for h in range(heads):
-            for c in range(2):
+            for c in range(3):
                 fcopy(h, c).start()
 
     srow = lax.broadcasted_iota(jnp.int32, (tokens, tokens), 0)
     tcol = lax.broadcasted_iota(jnp.int32, (tokens, tokens), 1)
     mask = srow <= tcol
 
+    loads[2].wait()
+    loads[3].wait()
+
+    def backward(h, _):
+        for c in range(3):
+            @pl.when(z < n - 1)
+            def _():
+                rcopy(h, c).wait_recv()
+
+            @pl.when((z > 0) & (z < n - 1))
+            def _():
+                rown[h, part(c)] = rown[h, part(c)] + rin[h, part(c)]
+                rcopy(h, c).start()
+
+        c = cols(h)
+        k = k_ref[:, c]
+        v = v_ref[:, c]
+        ph, pl_ = split(unpack(rin.at[h]))
+        qh, ql = split(rin[h, H + 8:])
+        kg_ref[:, c] = kg_ref[:, c] + (dot(v, qh) + dot(v, ql)) - (dot(k, ph) + dot(k, pl_))
+        vg_ref[:, c] = vg_ref[:, c] + (dot_t(k, qh) + dot_t(k, ql))
+        return 0
+
     def forward(h, _):
-        for c in range(2):
+        for c in range(3):
             @pl.when(z > 0)
             def _():
                 fcopy(h, c).wait_recv()
 
             @pl.when((z > 0) & (z < n - 1))
             def _():
-                fown[h, c] = fown[h, c] + fin[h, c]
+                fown[h, part(c)] = fown[h, part(c)] + fin[h, part(c)]
                 fcopy(h, c).start()
 
         c = cols(h)
@@ -120,12 +181,12 @@
         v = v_ref[:, c]
         kt = kt_ref[h]
         vt = vt_ref[h]
-        gt = gt_ref[h]
+        gt = g_ref[:, c].astype(F32).T.astype(BF16)
         ridge = ridge_ref[h]
         kk = jnp.concatenate([k, k], axis=1)
-        ghi, glo = split(fin[h, 0])
+        ghi, glo = split(unpack(fin.at[h]))
         gg = jnp.concatenate([ghi, ghi], axis=1)
-        m = fin[h, 1]
+        m = fin[h, H + 8:]
         mhi, mlo = split(m)
         mm = jnp.concatenate([mhi, mhi], axis=1)
         mt = m.T
@@ -170,12 +231,12 @@
         yy = jnp.concatenate([yh, yl], axis=0)
 
         cross = dot_t(yh, xh) + dot_t(yl, xh) + dot_t(yh, xl)
-        rown[h, 0] = cross + cross.T
-        rown[h, 1] = dot_t(gt, xh) + dot_t(gt, xl)
+        pack(rown.at[h], cross + cross.T)
+        rown[h, H + 8:] = dot_t(gt, xh) + dot_t(gt, xl)
 
         @pl.when(z == n - 1)
         def _():
-            for c2 in range(2):
+            for c2 in range(3):
                 rcopy(h, c2).start()
 
         ks = scores(xh, xx)
@@ -187,70 +248,63 @@
         kg_ref[:, c] = -(dot_t(ah, yh) + dot_t(al, yh) + dot_t(ah, yl)
                          + dot_t(bh, xh) + dot_t(bl, xh) + dot_t(bh, xl))
         vg_ref[:, c] = dot_t(ah, gt) + dot_t(al, gt)
+
+        @pl.when((z == n - 2) & (h >= LAG))
+        def _():
+            backward(h - LAG, 0)
+
         return 0
 
     lax.fori_loop(0, heads, forward, 0)
 
-    def backward(h, _):
-        for c in range(2):
+    lax.fori_loop(jnp.where(z == n - 2, max(heads - LAG, 0), 0), heads, backward, 0)
+
+    for h in range(heads):
+        for c in range(3):
             @pl.when(z < n - 1)
             def _():
-                rcopy(h, c).wait_recv()
-
-            @pl.when((z > 0) & (z < n - 1))
-            def _():
-                rown[h, c] = rown[h, c] + rin[h, c]
-                rcopy(h, c).start()
-
-        c = cols(h)
-        k = k_ref[:, c]
-        v = v_ref[:, c]
-        ph, pl_ = split(rin[h, 0])
-        qh, ql = split(rin[h, 1])
-        kg_ref[:, c] = kg_ref[:, c] + (dot(v, qh) + dot(v, ql)) - (dot(k, ph) + dot(k, pl_))
-        vg_ref[:, c] = vg_ref[:, c] + (dot_t(k, qh) + dot_t(k, ql))
-        return 0
-
-    lax.fori_loop(0, heads, backward, 0)
-
-    for h in range(heads):
-        for c in range(2):
-            @pl.when(z < n - 1)
-            def _():
                 fcopy(h, c).wait_send()
 
             @pl.when(z > 0)
             def _():
                 rcopy(h, c).wait_send()
+
+
+def store(*refs):
+    sems = refs[8]
+    copies = [pltpu.make_async_copy(refs[i], refs[i + 4], sems.at[i]) for i in range(4)]
+    for one in copies:
+        one.start()
+    for one in copies:
+        one.wait()
 
 
 def body(n, queries, keys, values, out_grad, ridge):
     tokens, width = queries.shape
     heads = width // D
+    hbm = pl.BlockSpec(memory_space=pltpu.HBM)
     vm = pl.BlockSpec(memory_space=pltpu.VMEM)
     out = jax.ShapeDtypeStruct((tokens, width), F32)
-    return pl.pallas_call(
+    parts = pl.pallas_call(
         functools.partial(kernel, n, heads),
         out_shape=[out] * 4,
-        in_specs=[pl.BlockSpec(memory_space=pltpu.SMEM)] + [vm] * 4,
+        in_specs=[pl.BlockSpec(memory_space=pltpu.SMEM)] + [hbm] * 4,
         out_specs=[vm] * 4,
         scratch_shapes=[
-            pltpu.VMEM((heads, D, tokens), BF16),
-            pltpu.VMEM((heads, D, tokens), BF16),
-            pltpu.VMEM((heads, D, tokens), BF16),
-            pltpu.VMEM((heads, 2, D, D), F32),
-            pltpu.VMEM((heads, 2, D, D), F32),
-            pltpu.VMEM((heads, 2, D, D), F32),
-            pltpu.VMEM((heads, 2, D, D), F32),
-            pltpu.SemaphoreType.DMA((heads, 2)),
-            pltpu.SemaphoreType.DMA((heads, 2)),
-            pltpu.SemaphoreType.DMA((heads, 2)),
-            pltpu.SemaphoreType.DMA((heads, 2)),
+            *[pltpu.VMEM((tokens, width), BF16)] * 4,
+            pltpu.SemaphoreType.DMA((4,)),
+            *[pltpu.VMEM((heads, D, tokens), BF16)] * 2,
+            *[pltpu.VMEM((heads, ROWS, D), F32)] * 4,
+            *[pltpu.SemaphoreType.DMA((heads, 3))] * 4,
         ],
         compiler_params=pltpu.CompilerParams(
-            collective_id=0, has_side_effects=True, vmem_limit_bytes=40 * 2**20),
+            collective_id=0, has_side_effects=True, vmem_limit_bytes=24 * 2**20),
         name="mesa",
     )(ridge, queries, keys, values, out_grad)
+    return pl.pallas_call(
+        store, out_shape=[out] * 4, in_specs=[vm] * 4, out_specs=[hbm] * 4,
+        scratch_shapes=[pltpu.SemaphoreType.DMA((4,))], name="store",
+    )(*parts)
 
 
 def solution(mesh):

time: 49.7 us -> 50.7 us (1.020)
  Pallas kernels: 41.2 us -> 42.1 us
    pallas_call x0 -> x1, Pallas kernels: none -> 2.86 us  [body(): pl.pallas_call(store, out_shape=[out] * 4, in_specs=[vm] * 4, out_specs=[...]
    pallas_call x1, Pallas kernels: 41.2 us -> 39.3 us  [body(): pl.pallas_call(functools.partial(kernel, n, heads), out_shape=[out] * 4,...]
    unnamed x14 -> x18, local copies, waits for them, and re-layouts: 7.62 us -> 7.62 us
where the time goes in v2:
time: 50.7 us; the launch traced here: 50.4 us
  Pallas kernels  42.1 us (83%)
  local copies, waits for them, and re-layouts  7.62 us (15%)
  between operations  0.66 us (1%)
    pallas_call x1, Pallas kernels, body(): pl.pallas_call(functools.partial(kernel, n, heads), out_shape=[out] * 4,...  39.3 us
    unnamed x18, local copies, waits for them, and re-layouts  7.62 us
    pallas_call x1, Pallas kernels, body(): pl.pallas_call(store, out_shape=[out] * 4, in_specs=[vm] * 4, out_specs=[...  2.86 us

profile of v2, /device:TPU:0, one launch (start us, length us, event | category | flops | bytes accessed | tf_op | source)
XLA Modules:
  0.0 50.4 jit_solution(17109254528686815299)
XLA Ops:
  0.6 0.0 copy-start.4
  0.6 0.9 %copy-done.4 = bf16[256,512]{1,0:T(8,128)(2,1)S(1)} copy-done((bf16[256,512]{1,0:T(8,128)(2,1)S(1)}, bf16[256,512]{1,0:T(8,128)(2,1)}, u32[]{:S(2)}) %copy-start.4) | copy-done | bytes 262168
  1.6 0.0 copy-start.5
  1.6 0.9 %copy-done.5 = bf16[256,512]{1,0:T(8,128)(2,1)S(1)} copy-done((bf16[256,512]{1,0:T(8,128)(2,1)S(1)}, bf16[256,512]{1,0:T(8,128)(2,1)}, u32[]{:S(2)}) %copy-start.5) | copy-done | bytes 262168
  2.5 0.0 copy-start.6
  2.5 0.9 %copy-done.6 = bf16[256,512]{1,0:T(8,128)(2,1)S(1)} copy-done((bf16[256,512]{1,0:T(8,128)(2,1)S(1)}, bf16[256,512]{1,0:T(8,128)(2,1)}, u32[]{:S(2)}) %copy-start.6) | copy-done | bytes 262168
  3.5 0.0 copy-start.7
  3.5 0.9 %copy-done.7 = bf16[256,512]{1,0:T(8,128)(2,1)S(1)} copy-done((bf16[256,512]{1,0:T(8,128)(2,1)S(1)}, bf16[256,512]{1,0:T(8,128)(2,1)}, u32[]{:S(2)}) %copy-start.7) | copy-done | bytes 262168
  4.4 0.0 copy-start.8
  4.4 0.7 %copy-done.8 = f32[4]{0:T(128)S(1)} copy-done((f32[4]{0:T(128)S(1)}, f32[4]{0:T(128)}, u32[]{:S(2)}) %copy-start.8) | copy-done | bytes 40
  5.1 39.3 %mesa.1 = (f32[256,512]{1,0:T(8,128)S(1)}, f32[256,512]{1,0:T(8,128)S(1)}, f32[256,512]{1,0:T(8,128)S(1)}, f32[256,512]{1,0:T(8,128)S(1)}) custom-call(f32[4]{0:T(128)S(1)} %copy-done.8, bf16[256,512]{1,0:T(8,128)(2,1)S(1)} %copy-done.4, bf16[256,512]{1,0:T(8,128)(2,1)S(1)} %copy-done.5, bf16[256,512]{1,0:T(8,128)(2,1)S(1)} %copy-done.6, ...), custom_call_target="tpu_custom_call" | custom-call | tf_op jit(solution)/shard_map/mesa/pallas_call | solution.py:288
  44.4 0.0 copy-start
  44.4 0.8 %copy-done = f32[256,512]{1,0:T(8,128)} copy-done((f32[256,512]{1,0:T(8,128)}, f32[256,512]{1,0:T(8,128)S(1)}, u32[]{:S(2)}) %copy-start) | copy-done | bytes 524312
  45.2 0.0 copy-start.1
  45.2 0.8 %copy-done.1 = f32[256,512]{1,0:T(8,128)} copy-done((f32[256,512]{1,0:T(8,128)}, f32[256,512]{1,0:T(8,128)S(1)}, u32[]{:S(2)}) %copy-start.1) | copy-done | bytes 524312
  45.9 0.0 copy-start.2
  45.9 0.8 %copy-done.2 = f32[256,512]{1,0:T(8,128)} copy-done((f32[256,512]{1,0:T(8,128)}, f32[256,512]{1,0:T(8,128)S(1)}, u32[]{:S(2)}) %copy-start.2) | copy-done | bytes 524312
  46.8 0.0 copy-start.3
  46.8 0.8 %copy-done.3 = f32[256,512]{1,0:T(8,128)} copy-done((f32[256,512]{1,0:T(8,128)}, f32[256,512]{1,0:T(8,128)S(1)}, u32[]{:S(2)}) %copy-start.3) | copy-done | bytes 524312
  47.5 2.9 %store.1 = (f32[256,512]{1,0:T(8,128)}, f32[256,512]{1,0:T(8,128)}, f32[256,512]{1,0:T(8,128)}, f32[256,512]{1,0:T(8,128)}) custom-call(f32[256,512]{1,0:T(8,128)} %copy-done, f32[256,512]{1,0:T(8,128)} %copy-done.1, f32[256,512]{1,0:T(8,128)} %copy-done.2, f32[256,512]{1,0:T(8,128)} %copy-done.3), custom_call_target="tpu_custom_call" | custom-call | tf_op jit(solution)/shard_map/store/pallas_call | solution.py:304
Async XLA Ops:
  0.6 1.0 %copy-start.4 = (bf16[256,512]{1,0:T(8,128)(2,1)S(1)}, bf16[256,512]{1,0:T(8,128)(2,1)}, u32[]{:S(2)}) copy-start(bf16[256,512]{1,0:T(8,128)(2,1)} %q_hbm.1) | copy-start | bytes 786436
  1.6 0.9 %copy-start.5 = (bf16[256,512]{1,0:T(8,128)(2,1)S(1)}, bf16[256,512]{1,0:T(8,128)(2,1)}, u32[]{:S(2)}) copy-start(bf16[256,512]{1,0:T(8,128)(2,1)} %k_hbm.1) | copy-start | bytes 786436
  2.5 0.9 %copy-start.6 = (bf16[256,512]{1,0:T(8,128)(2,1)S(1)}, bf16[256,512]{1,0:T(8,128)(2,1)}, u32[]{:S(2)}) copy-start(bf16[256,512]{1,0:T(8,128)(2,1)} %v_hbm.1) | copy-start | bytes 786436
  3.5 0.9 %copy-start.7 = (bf16[256,512]{1,0:T(8,128)(2,1)S(1)}, bf16[256,512]{1,0:T(8,128)(2,1)}, u32[]{:S(2)}) copy-start(bf16[256,512]{1,0:T(8,128)(2,1)} %g_hbm.1) | copy-start | bytes 786436
  4.4 0.7 %copy-start.8 = (f32[4]{0:T(128)S(1)}, f32[4]{0:T(128)}, u32[]{:S(2)}) copy-start(f32[4]{0:T(128)} %ridge_ref.1) | copy-start | bytes 52
  44.4 0.8 %copy-start = (f32[256,512]{1,0:T(8,128)}, f32[256,512]{1,0:T(8,128)S(1)}, u32[]{:S(2)}) copy-start(f32[256,512]{1,0:T(8,128)S(1)} %get-tuple-element.8.refs_0_) | copy-start | bytes 1572868
  45.2 0.8 %copy-start.1 = (f32[256,512]{1,0:T(8,128)}, f32[256,512]{1,0:T(8,128)S(1)}, u32[]{:S(2)}) copy-start(f32[256,512]{1,0:T(8,128)S(1)} %get-tuple-element.9.refs_1_) | copy-start | bytes 1572868
  45.9 0.8 %copy-start.2 = (f32[256,512]{1,0:T(8,128)}, f32[256,512]{1,0:T(8,128)S(1)}, u32[]{:S(2)}) copy-start(f32[256,512]{1,0:T(8,128)S(1)} %get-tuple-element.10.refs_2_) | copy-start | bytes 1572868
  46.8 0.8 %copy-start.3 = (f32[256,512]{1,0:T(8,128)}, f32[256,512]{1,0:T(8,128)S(1)}, u32[]{:S(2)}) copy-start(f32[256,512]{1,0:T(8,128)S(1)} %get-tuple-element.11.refs_3_) | copy-start | bytes 1572868

commit v3 on v2

--- a/solution.py
+++ b/solution.py
@@ -64,7 +64,8 @@
 
 
 def kernel(n, heads, ridge_ref, q_hbm, k_hbm, v_hbm, g_hbm,
-           out_ref, qg_ref, kg_ref, vg_ref,
+           out_hbm, qg_hbm, kg_hbm, vg_hbm,
+           out_ref, qg_ref, kg_ref, vg_ref, stored,
            q_ref, k_ref, v_ref, g_ref, load, kt_ref, vt_ref, fown, fin, rown, rin,
            fsend, frecv, rsend, rrecv):
     z = lax.axis_index("seq")
@@ -85,6 +86,10 @@
 
     def cols(h):
         return pl.ds(pl.multiple_of(h * D, D), D)
+
+    def save(i, h):
+        a, b = ((out_ref, out_hbm), (qg_ref, qg_hbm), (kg_ref, kg_hbm), (vg_ref, vg_hbm))[i]
+        return pltpu.make_async_copy(a.at[:, cols(h)], b.at[:, cols(h)], stored.at[i, h])
 
     def part(c):
         return pl.ds(*CHUNKS[c])
@@ -163,6 +168,8 @@
         qh, ql = split(rin[h, H + 8:])
         kg_ref[:, c] = kg_ref[:, c] + (dot(v, qh) + dot(v, ql)) - (dot(k, ph) + dot(k, pl_))
         vg_ref[:, c] = vg_ref[:, c] + (dot_t(k, qh) + dot_t(k, ql))
+        save(2, h).start()
+        save(3, h).start()
         return 0
 
     def forward(h, _):
@@ -225,6 +232,7 @@
 
         x, y = state[0][0], state[1][0]
         qg_ref[:, c] = y.T
+        save(1, h).start()
         xh, xl = split(x)
         yh, yl = split(y)
         xx = jnp.concatenate([xh, xl], axis=0)
@@ -243,6 +251,7 @@
         ah, al = split(ks)
         out = dot(mm, xx) + dot(mlo, xh) + dot(vt, ah) + dot(vt, al)
         out_ref[:, c] = out.T
+        save(0, h).start()
         ka = scores(yh, yy) - vs
         bh, bl = split(ka)
         kg_ref[:, c] = -(dot_t(ah, yh) + dot_t(al, yh) + dot_t(ah, yl)
@@ -260,6 +269,8 @@
     lax.fori_loop(jnp.where(z == n - 2, max(heads - LAG, 0), 0), heads, backward, 0)
 
     for h in range(heads):
+        for i in range(4):
+            save(i, h).wait()
         for c in range(3):
             @pl.when(z < n - 1)
             def _():
@@ -282,15 +293,16 @@
 def body(n, queries, keys, values, out_grad, ridge):
     tokens, width = queries.shape
     heads = width // D
-    hbm = pl.BlockSpec(memory_space=pltpu.HBM)
-    vm = pl.BlockSpec(memory_space=pltpu.VMEM)
+    hbm = pl.BlockSpec(memory_space=pl.ANY)
     out = jax.ShapeDtypeStruct((tokens, width), F32)
     parts = pl.pallas_call(
         functools.partial(kernel, n, heads),
         out_shape=[out] * 4,
         in_specs=[pl.BlockSpec(memory_space=pltpu.SMEM)] + [hbm] * 4,
-        out_specs=[vm] * 4,
+        out_specs=[hbm] * 4,
         scratch_shapes=[
+            *[pltpu.VMEM((tokens, width), F32)] * 4,
+            pltpu.SemaphoreType.DMA((4, heads)),
             *[pltpu.VMEM((tokens, width), BF16)] * 4,
             pltpu.SemaphoreType.DMA((4,)),
             *[pltpu.VMEM((heads, D, tokens), BF16)] * 2,
@@ -298,11 +310,11 @@
             *[pltpu.SemaphoreType.DMA((heads, 3))] * 4,
         ],
         compiler_params=pltpu.CompilerParams(
-            collective_id=0, has_side_effects=True, vmem_limit_bytes=24 * 2**20),
+            collective_id=0, has_side_effects=True, vmem_limit_bytes=56 * 2**20),
         name="mesa",
     )(ridge, queries, keys, values, out_grad)
     return pl.pallas_call(
-        store, out_shape=[out] * 4, in_specs=[vm] * 4, out_specs=[hbm] * 4,
+        store, out_shape=[out] * 4, in_specs=[hbm] * 4, out_specs=[hbm] * 4,
         scratch_shapes=[pltpu.SemaphoreType.DMA((4,))], name="store",
     )(*parts)
 

time: 50.7 us -> 106 us (2.09)
  Pallas kernels: 42.1 us -> 105 us
  local copies, waits for them, and re-layouts: 7.62 us -> 0 us
    pallas_call x1, Pallas kernels: 2.86 us -> 64.7 us  [body(): pl.pallas_call(store, out_shape=[out] * 4, in_specs=[hbm] * 4, out_specs=...]
    unnamed x18 -> x0, local copies, waits for them, and re-layouts: 7.62 us -> none
where the time goes in v3:
time: 106 us
  Pallas kernels  105 us (99%)
    pallas_call x1, Pallas kernels, body(): pl.pallas_call(store, out_shape=[out] * 4, in_specs=[hbm] * 4, out_specs=...  64.7 us
    pallas_call x1, Pallas kernels, body(): pl.pallas_call(functools.partial(kernel, n, heads), out_shape=[out] * 4,...  40.2 us

profile of v3, /device:TPU:0, one launch (start us, length us, event | category | flops | bytes accessed | tf_op | source)
XLA Modules:
  0.0 105.6 jit_solution(17414851306070935180)
XLA Ops:
  0.6 40.2 %mesa.1 = (f32[256,512]{1,0:T(8,128)}, f32[256,512]{1,0:T(8,128)}, f32[256,512]{1,0:T(8,128)}, f32[256,512]{1,0:T(8,128)}) custom-call(f32[4]{0:T(128)} %ridge_ref.1, bf16[256,512]{1,0:T(8,128)(2,1)} %q_hbm.1, bf16[256,512]{1,0:T(8,128)(2,1)} %k_hbm.1, bf16[256,512]{1,0:T(8,128)(2,1)} %v_hbm.1, bf16[256,512]{1,0:T(8,128)(2,1)} %g_hbm.1), custom_call_target="tpu_custom_call" | custom-call | tf_op jit(solution)/shard_map/mesa/pallas_call | solution.py:298
  40.9 64.7 %store.1 = (f32[256,512]{1,0:T(8,128)}, f32[256,512]{1,0:T(8,128)}, f32[256,512]{1,0:T(8,128)}, f32[256,512]{1,0:T(8,128)}) custom-call(f32[256,512]{1,0:T(8,128)} %get-tuple-element.8.refs_0_, f32[256,512]{1,0:T(8,128)} %get-tuple-element.9.refs_1_, f32[256,512]{1,0:T(8,128)} %get-tuple-element.10.refs_2_, f32[256,512]{1,0:T(8,128)} %get-tuple-element.11.refs_3_), custom_call_target="tpu_custom_call" | custom-call | tf_op jit(solution)/shard_map/store/pallas_call | solution.py:316

commit v4 on v3

--- a/solution.py
+++ b/solution.py
@@ -294,6 +294,7 @@
     tokens, width = queries.shape
     heads = width // D
     hbm = pl.BlockSpec(memory_space=pl.ANY)
+    vm = pl.BlockSpec(memory_space=pltpu.VMEM)
     out = jax.ShapeDtypeStruct((tokens, width), F32)
     parts = pl.pallas_call(
         functools.partial(kernel, n, heads),
@@ -314,7 +315,7 @@
         name="mesa",
     )(ridge, queries, keys, values, out_grad)
     return pl.pallas_call(
-        store, out_shape=[out] * 4, in_specs=[hbm] * 4, out_specs=[hbm] * 4,
+        store, out_shape=[out] * 4, in_specs=[vm] * 4, out_specs=[hbm] * 4,
         scratch_shapes=[pltpu.SemaphoreType.DMA((4,))], name="store",
     )(*parts)
 

time: 106 us -> 43.9 us (0.41)
  Pallas kernels: 105 us -> 43.1 us
    pallas_call x1, Pallas kernels: 64.7 us -> 2.86 us  [body(): pl.pallas_call(store, out_shape=[out] * 4, in_specs=[vm] * 4, out_specs=[...]
where the time goes in v4:
time: 43.9 us; the launch traced here: 43.7 us
  Pallas kernels  43.1 us (98%)
  between operations  0.64 us (1%)
    pallas_call x1, Pallas kernels, body(): pl.pallas_call(functools.partial(kernel, n, heads), out_shape=[out] * 4,...  40.2 us
    pallas_call x1, Pallas kernels, body(): pl.pallas_call(store, out_shape=[out] * 4, in_specs=[vm] * 4, out_specs=[...  2.86 us

profile of v4, /device:TPU:0, one launch (start us, length us, event | category | flops | bytes accessed | tf_op | source)
XLA Modules:
  0.0 43.7 jit_solution(13717871433941437645)
XLA Ops:
  0.6 40.2 %mesa.1 = (f32[256,512]{1,0:T(8,128)}, f32[256,512]{1,0:T(8,128)}, f32[256,512]{1,0:T(8,128)}, f32[256,512]{1,0:T(8,128)}) custom-call(f32[4]{0:T(128)} %ridge_ref.1, bf16[256,512]{1,0:T(8,128)(2,1)} %q_hbm.1, bf16[256,512]{1,0:T(8,128)(2,1)} %k_hbm.1, bf16[256,512]{1,0:T(8,128)(2,1)} %v_hbm.1, bf16[256,512]{1,0:T(8,128)(2,1)} %g_hbm.1), custom_call_target="tpu_custom_call" | custom-call | tf_op jit(solution)/shard_map/mesa/pallas_call | solution.py:299
  40.9 2.9 %store.1 = (f32[256,512]{1,0:T(8,128)}, f32[256,512]{1,0:T(8,128)}, f32[256,512]{1,0:T(8,128)}, f32[256,512]{1,0:T(8,128)}) custom-call(f32[256,512]{1,0:T(8,128)} %get-tuple-element.8.refs_0_, f32[256,512]{1,0:T(8,128)} %get-tuple-element.9.refs_1_, f32[256,512]{1,0:T(8,128)} %get-tuple-element.10.refs_2_, f32[256,512]{1,0:T(8,128)} %get-tuple-element.11.refs_3_), custom_call_target="tpu_custom_call" | custom-call | tf_op jit(solution)/shard_map/store/pallas_call | solution.py:317
